TPU v7x, 512 devices: a whole 4x8x8 slice. The times are simulated.
512 devices in a mesh: rows: 8 (over z), cols: 8 (over y), depth: 8 (over x, core).
Axes of the slice: x: 4, y: 8, z: 8, core: 2. Of those that a mesh axis runs over, the one named last changes fastest.
Arguments:
- tokens: bfloat16 [512, 12288], P(('rows', 'cols'), 'depth'), may hold values from -6 to 6
- weight_in: bfloat16 [12288, 49152], P('depth', ('rows', 'cols')), may hold values from -0.0546875 to 0.0546875
- bias_in: float32 [49152], P(('rows', 'cols')), may hold values from -4 to 4
- weight_out: bfloat16 [49152, 12288], P(('rows', 'cols'), 'depth'), may hold values from -0.02734375 to 0.02734375
- bias_out: float32 [12288], P('depth'), may hold values from -3 to 3
Outputs:
- output: bfloat16 [512, 12288], P(('rows', 'cols'), 'depth')
All inputs are finite; a program needn't handle non-finite values.
Results may differ from a plain program's by a relative error of at most 0.0046.
Values may be sent and summed in bfloat16 or wider, within the bound.
No kernel may reach another device: no remote copies, remote signals or barrier semaphores. Data moves between devices by JAX's collectives and lax.ppermute only.
A program may use at most 64 MiB of HBM per device.

v0:
```python
import jax
import jax.numpy as jnp
from jax import lax
from jax.sharding import PartitionSpec as P


def shards(tokens, weight_in, bias_in, weight_out, bias_out):
    partial_value = jnp.dot(
        lax.all_gather(tokens, ("rows", "cols"), axis=0, tiled=True),
        weight_in,
        preferred_element_type=jnp.float32,
    )
    total = lax.psum(partial_value, "depth")
    active = jax.nn.gelu(total + bias_in, approximate=True).astype(jnp.bfloat16)
    summed = lax.psum_scatter(
        jnp.dot(active, weight_out, preferred_element_type=jnp.float32),
        ("rows", "cols"),
        scatter_dimension=0,
        tiled=True,
    )
    return (summed + bias_out).astype(jnp.bfloat16)


def solution(mesh):
    in_specs = (
        P(("rows", "cols"), "depth"),
        P("depth", ("rows", "cols")),
        P(("rows", "cols")),
        P(("rows", "cols"), "depth"),
        P("depth"),
    )
    out_specs = P(("rows", "cols"), "depth")
    return jax.shard_map(shards, mesh=mesh, in_specs=in_specs, out_specs=out_specs, check_vma=False)
```

profile of v0, /device:TPU:6, one launch (start us, length us, event | category | flops | bytes accessed | tf_op | source)
XLA Modules:
  0.0 353.3 jit_solution(1478955682102614328)
XLA Ops:
  6.5 0.0 copy-start
  6.5 0.0 all-gather.2.cloned.1.call-start
  6.5 0.7 all-gather.2.cloned.1.call-update
  7.3 0.0 all-reduce.4.cloned.1.call-start
  7.3 90.5 %all-gather.2.cloned.1.call-done = bf16[512,1536]{1,0:T(8,128)(2,1)} async-done(((bf16[8,1536]{1,0:T(8,128)(2,1)}), bf16[512,1536]{1,0:T(8,128)(2,1)}) %all-gather.2.cloned.1.call-update) | async-done | bytes 1572880 | tf_op jit(solution)/shard_map/all_gather | solution.py:9
  97.8 4.7 %fusion.20 = f32[512,768]{1,0:T(8,128)} fusion(bf16[512,1536]{1,0:T(8,128)(2,1)} %all-gather.2.cloned.1.call-done, bf16[1536,768]{1,0:T(8,128)(2,1)} %param.6), kind=kOutput, calls=%fused_computation.21 | convolution fusion | flops 1207959552 | bytes 5505024 | tf_op jit(solution)/shard_map/dot_general | solution.py:8
  102.5 0.0 copy-start.2
  102.5 0.0 all-reduce.4.cloned.1.call-update
  102.5 0.0 all-reduce.6.cloned.1.call-start
  102.5 69.4 %all-reduce.4.cloned.1.call-done = f32[512,768]{1,0:T(8,128)} async-done(((f32[512,768]{1,0:T(8,128)}), f32[512,768]{1,0:T(8,128)}) %all-reduce.4.cloned.1.call-update) | async-done | bytes 1572880 | tf_op jit(solution)/shard_map/psum | solution.py:13
  172.0 0.0 copy-done
  172.0 0.0 copy-done.2
  172.0 4.6 %fusion.8 = f32[512,1536]{1,0:T(8,128)} fusion(bf16[768,1536]{1,0:T(8,128)(2,1)S(1)} %copy-done, f32[512,768]{1,0:T(8,128)} %all-reduce.4.cloned.1.call-done, f32[768]{0:T(1024)S(1)} %copy-done.2), kind=kOutput, calls=%fused_computation.9 | convolution fusion | flops 1211891712 | bytes 7080960 | tf_op jit(solution)/shard_map/dot_general | solution.py:16
  176.6 0.0 copy-start.1
  176.6 0.0 all-reduce.6.cloned.1.call-update
  176.6 1.3 dynamic-slice
  178.5 166.8 %all-reduce.6.cloned.1.call-done = f32[512,1536]{1,0:T(8,128)} async-done(((f32[512,1536]{1,0:T(8,128)}), f32[512,1536]{1,0:T(8,128)}) %all-reduce.6.cloned.1.call-update) | async-done | bytes 3145744
  345.3 0.0 copy-done.1
  345.3 1.4 fusion.15
Async XLA Ops:
  6.5 165.4 %copy-start = (bf16[768,1536]{1,0:T(8,128)(2,1)S(1)}, bf16[768,1536]{1,0:T(8,128)(2,1)}, u32[]{:S(2)}) copy-start(bf16[768,1536]{1,0:T(8,128)(2,1)} %param.8) | copy-start | bytes 7077892
  6.5 91.2 %all-gather.2.cloned.1.call-start = ((), (), s32[]{:S(2)}) async-start(), calls=%async_computation | async-start | bytes 1597440 | tf_op jit(solution)/shard_map/all_gather | solution.py:9
  7.3 164.7 %all-reduce.4.cloned.1.call-start = ((), (), s32[]{:S(2)}) async-start(), calls=%async_computation.1 | async-start | bytes 3145728 | tf_op jit(solution)/shard_map/psum | solution.py:13
  102.5 69.5 %copy-start.2 = (f32[768]{0:T(1024)S(1)}, f32[768]{0:T(1024)}, u32[]{:S(2)}) copy-start(f32[768]{0:T(1024)} %param.7) | copy-start | bytes 9220
  102.5 242.8 %all-reduce.6.cloned.1.call-start = ((), (), s32[]{:S(2)}) async-start(), calls=%async_computation.2 | async-start | bytes 6291456
  176.6 168.8 %copy-start.1 = (f32[1536]{0:T(1024)S(1)}, f32[1536]{0:T(1024)}, u32[]{:S(2)}) copy-start(f32[1536]{0:T(1024)} %param.9) | copy-start | bytes 18436
Sparse Core Ops, SparseCore 0:
  10.4 87.3 all-gather.1
  102.6 69.3 all-reduce.3
  176.7 168.5 all-reduce.5
where the time goes:
time: 354 us; the launch traced here: 353 us
  waiting for transfers between devices  327 us (92%)
  between operations  13.8 us (4%)
  matrix products  9.27 us (3%)
    unnamed x4, waiting for transfers between devices  168 us
    all_gather x1, waiting for transfers between devices, shards(): lax.all_gather(tokens, ('rows', 'cols'), axis=0, tiled=True)  90.5 us
    psum x1, waiting for transfers between devices, shards(): total = lax.psum(partial_value, 'depth')  69.4 us
  transfers between devices with their start and end apart: 3, of which 3 were waited for; matrix products, arithmetic and copies ran while one was open for 0% of the time, Pallas kernels for 0%

commit v1 on v0

v1 whole, which is shorter than its diff:
```python
import jax
import jax.numpy as jnp
from jax import lax
from jax.sharding import PartitionSpec as P

PLANE = ("rows", "cols")


def shards(tokens, weight_in, bias_in, weight_out, bias_out):
    own = tokens.shape[0]
    planes = lax.axis_size(PLANE)
    gathered = lax.all_to_all(
        jnp.broadcast_to(tokens[None], (planes,) + tokens.shape), PLANE, 0, 0
    ).reshape(planes * own, -1)
    partial_hidden = jnp.dot(gathered, weight_in, preferred_element_type=jnp.float32)
    depths = lax.axis_size("depth")
    pieces = lax.all_to_all(
        partial_hidden.astype(jnp.bfloat16).reshape(depths, -1, weight_in.shape[1]),
        "depth", 0, 0,
    )
    hidden = jnp.sum(pieces.astype(jnp.float32), axis=0) + bias_in
    active = jax.nn.gelu(hidden, approximate=True).astype(jnp.bfloat16)
    active = lax.all_gather(active, "depth", axis=0, tiled=True)
    partial_out = jnp.dot(active, weight_out, preferred_element_type=jnp.float32)
    parts = lax.all_to_all(
        partial_out.astype(jnp.bfloat16).reshape(planes, own, -1), PLANE, 0, 0
    )
    summed = jnp.sum(parts.astype(jnp.float32), axis=0)
    return (summed + bias_out).astype(jnp.bfloat16)


def solution(mesh):
    in_specs = (
        P(("rows", "cols"), "depth"),
        P("depth", ("rows", "cols")),
        P(("rows", "cols")),
        P(("rows", "cols"), "depth"),
        P("depth"),
    )
    out_specs = P(("rows", "cols"), "depth")
    return jax.shard_map(shards, mesh=mesh, in_specs=in_specs, out_specs=out_specs, check_vma=False)
```

time: 354 us -> 143 us (0.40)
  waiting for transfers between devices: 327 us -> 0 us
  blocking collectives: 0 us -> 136 us
  between operations: 13.8 us -> 0.06 us
  matrix products: 9.27 us -> 2.76 us
    unnamed x4 -> x0, waiting for transfers between devices: 168 us -> none
    all_to_all x0 -> x3, blocking collectives: none -> 123 us  [the longest x1 57.8 us: shards(): lax.all_to_all(jnp.broadcast_to(tokens[None], (planes,) + tokens.shape),...]
    all_gather x1 -> x0, waiting for transfers between devices: 90.5 us -> none  [shards(): lax.all_gather(tokens, ('rows', 'cols'), axis=0, tiled=True)]
    psum x1 -> x0, waiting for transfers between devices: 69.4 us -> none  [shards(): total = lax.psum(partial_value, 'depth')]
    all_gather x0 -> x1, blocking collectives: none -> 13.5 us  [shards(): active = lax.all_gather(active, 'depth', axis=0, tiled=True)]
  transfers between devices with their start and end apart: 3 -> 0, of which waited for: 3 -> 0; matrix products, arithmetic and copies ran while one was open for 0% -> 0% of each run, Pallas kernels for 0% -> 0%
where the time goes in v1:
time: 143 us; the launch traced here: 141 us
  blocking collectives  136 us (95%)
  matrix products  2.76 us (2%)
  local copies, waits for them, and re-layouts  1.45 us (1%)
    all_to_all x1, blocking collectives, shards(): lax.all_to_all(jnp.broadcast_to(tokens[None], (planes,) + tokens.shape),...  57.8 us
    all_to_all x1, blocking collectives, shards(): lax.all_to_all(partial_out.astype(jnp.bfloat16).reshape(planes, own, -1),...  49.1 us
    all_to_all x1, blocking collectives, shards(): lax.all_to_all(partial_hidden.astype(jnp.bfloat16).reshape(depths, -1, we...  15.8 us
    all_gather x1, blocking collectives, shards(): active = lax.all_gather(active, 'depth', axis=0, tiled=True)  13.5 us

profile of v1, /device:TPU:6, one launch (start us, length us, event | category | flops | bytes accessed | tf_op | source)
XLA Modules:
  0.0 141.5 jit_solution(7724320758658860799)
XLA Ops:
  0.0 0.0 copy-start
  0.0 1.0 broadcast_in_dim.2
  1.0 0.0 copy-start.3
  1.0 57.8 %all_to_all.15 = bf16[64,8,1536]{2,1,0:T(8,128)(2,1)S(1)} all-to-all(bf16[64,8,1536]{2,1,0:T(8,128)(2,1)S(1)} %broadcast_in_dim.2), channel_id=1, replica_groups=mesh['rows'=8,'cols'=8,'depth'=8] {'rows','cols'}, dimensions={0} | all-to-all | bytes 3145728 | tf_op jit(solution)/shard_map/all_to_all | solution.py:12
  58.8 0.0 copy-done.3
  58.8 1.4 fusion.3
  60.2 0.0 copy-start.2
  60.2 15.8 %all_to_all.16 = bf16[8,64,768]{2,1,0:T(8,128)(2,1)S(1)} all-to-all(bf16[8,64,768]{2,1,0:T(8,128)(2,1)S(1)} %bitcast.11), channel_id=1, replica_groups=mesh['rows'=8,'cols'=8,'depth'=8] {'depth'}, dimensions={0} | all-to-all | bytes 1572864 | tf_op jit(solution)/shard_map/all_to_all | solution.py:17
  76.0 0.1 convert_reduce_fusion.1
  76.1 0.0 copy-done.2
  76.1 0.1 fusion.13
  76.2 13.5 %all_gather.3 = bf16[512,768]{1,0:T(8,128)(2,1)S(1)} all-gather(bf16[64,768]{1,0:T(8,128)(2,1)S(1)} %fusion.13), channel_id=1, replica_groups=mesh['rows'=8,'cols'=8,'depth'=8] {'depth'}, dimensions={0}, use_global_device_ids=true | all-gather | bytes 884736 | tf_op jit(solution)/shard_map/all_gather | solution.py:23
  89.6 0.0 copy-done
  89.6 1.4 fusion
  91.0 49.1 %all_to_all.17 = bf16[64,8,1536]{2,1,0:T(8,128)(2,1)S(1)} all-to-all(bf16[64,8,1536]{2,1,0:T(8,128)(2,1)S(1)} %fusion), channel_id=1, replica_groups=mesh['rows'=8,'cols'=8,'depth'=8] {'rows','cols'}, dimensions={0} | all-to-all | bytes 3145728 | tf_op jit(solution)/shard_map/all_to_all | solution.py:25
  140.2 0.0 copy-start.1
  140.2 0.2 convert_reduce_fusion
  140.4 0.4 copy-done.1
  140.9 0.6 add_convert_fusion
Async XLA Ops:
  0.0 89.6 %copy-start = (bf16[768,1536]{1,0:T(8,128)(2,1)S(1)}, bf16[768,1536]{1,0:T(8,128)(2,1)}, u32[]{:S(2)}) copy-start(bf16[768,1536]{1,0:T(8,128)(2,1)} %param.8) | copy-start | bytes 7077892
  1.0 57.8 %copy-start.3 = (bf16[1536,768]{1,0:T(8,128)(2,1)S(1)}, bf16[1536,768]{1,0:T(8,128)(2,1)}, u32[]{:S(2)}) copy-start(bf16[1536,768]{1,0:T(8,128)(2,1)} %param.6) | copy-start | bytes 7077892
  60.2 15.9 %copy-start.2 = (f32[768]{0:T(1024)S(1)}, f32[768]{0:T(1024)}, u32[]{:S(2)}) copy-start(f32[768]{0:T(1024)} %param.7) | copy-start | bytes 9220
  140.2 0.7 copy-start.1

commit v2 on v0

v2 whole, which is shorter than its diff:
```python
import jax
import jax.numpy as jnp
from jax import lax
from jax.sharding import PartitionSpec as P

PLANE = ("rows", "cols")
ALL = ("rows", "cols", "depth")


def parity_groups(n_rows, n_cols):
    return [
        [r * n_cols + c for r in range(p, n_rows, 2) for c in range(q, n_cols, 2)]
        for p in range(2)
        for q in range(2)
    ]


def square_groups(n_rows, n_cols, n_depth):
    groups = []
    for d in range(n_depth):
        for r in range(d % 2, n_rows + d % 2, 2):
            for c in range(d % 2, n_cols + d % 2, 2):
                chips = [(i % n_rows, j % n_cols) for i in (r, r + 1) for j in (c, c + 1)]
                chips.sort(key=lambda chip: (chip[0] % 2, chip[1] % 2))
                groups.append([(i * n_cols + j) * n_depth + d for i, j in chips])
    return groups


def swap_cores(x):
    return lax.ppermute(x, "depth", [(d, d ^ 1) for d in range(lax.axis_size("depth"))])


def swap_chips(x, stage):
    n = lax.axis_size("depth")
    pairs = []
    for d in range(n):
        chip, core = d // 2, d % 2
        step = 1 if (chip + core + stage) % 2 == 0 else -1
        pairs.append((d, ((chip + step) * 2 + core) % n))
    return lax.ppermute(x, "depth", pairs)


def shards(tokens, weight_in, bias_in, weight_out, bias_out):
    own, width = tokens.shape
    n_rows, n_cols, n_depth = (lax.axis_size(a) for a in ALL)
    far, near = parity_groups(n_rows, n_cols), square_groups(n_rows, n_cols, n_depth)
    members = n_rows * n_cols // 4
    quarter = members * own
    f32, bf16 = jnp.float32, jnp.bfloat16
    first = lax.axis_index("depth") % 2 == 0
    tokens, first = lax.optimization_barrier((tokens, first))

    def repeat(x, n):
        return jnp.broadcast_to(x[None], (n,) + x.shape)

    def add(x):
        x = x.astype(f32)
        return (x[0] + x[1]) + (x[2] + x[3])

    mine = lax.all_to_all(repeat(tokens, members), PLANE, 0, 0, axis_index_groups=far).reshape(quarter, width)
    full = lax.all_to_all(repeat(mine, 4), ALL, 0, 0, axis_index_groups=near).reshape(-1, width)
    partial = jnp.dot(full, weight_in, preferred_element_type=f32)

    partial = partial.reshape(4, 2, quarter // 2, -1)
    keep = jnp.where(first, partial[:, 0], partial[:, 1])
    send = jnp.where(first, partial[:, 1], partial[:, 0])
    total = keep + swap_cores(send)
    for stage in range(2):
        total = total + swap_chips(total.astype(bf16), stage).astype(f32)
    ours = jax.nn.gelu(total + bias_in, approximate=True).astype(bf16)
    theirs = swap_cores(ours)
    active = jnp.stack([jnp.where(first, ours, theirs), jnp.where(first, theirs, ours)], axis=1)
    active = active.reshape(4 * quarter, -1)

    outs = jnp.dot(active, weight_out, preferred_element_type=f32).astype(bf16)
    total = add(lax.all_to_all(outs.reshape(4, quarter, width), ALL, 0, 0, axis_index_groups=near))
    parts = lax.all_to_all(total.astype(bf16).reshape(members, own, width), PLANE, 0, 0, axis_index_groups=far)
    return (jnp.sum(parts.astype(f32), axis=0) + bias_out).astype(bf16)


def solution(mesh):
    in_specs = (
        P(("rows", "cols"), "depth"),
        P("depth", ("rows", "cols")),
        P(("rows", "cols")),
        P(("rows", "cols"), "depth"),
        P("depth"),
    )
    out_specs = P(("rows", "cols"), "depth")
    return jax.shard_map(shards, mesh=mesh, in_specs=in_specs, out_specs=out_specs, check_vma=False)
```

time: 354 us -> 123 us (0.35)
  waiting for transfers between devices: 327 us -> 19 us
  blocking collectives: 0 us -> 87.6 us
  between operations: 13.8 us -> 0.16 us
  starting transfers between devices: 0.08 us -> 9.29 us
  matrix products: 9.27 us -> 2.76 us
    unnamed x4 -> x0, waiting for transfers between devices: 168 us -> none
    all_gather x1 -> x0, waiting for transfers between devices: 90.5 us -> none  [shards(): lax.all_gather(tokens, ('rows', 'cols'), axis=0, tiled=True)]
    all_to_all x0 -> x4, blocking collectives: none -> 87.6 us  [the longest x1 32.2 us: shards(): lax.all_to_all(repeat(tokens, members), PLANE, 0, 0, axis_index_groups=far)]
    psum x1 -> x0, waiting for transfers between devices: 69.4 us -> none  [shards(): total = lax.psum(partial_value, 'depth')]
    ppermute x0 -> x4, waiting for transfers between devices: none -> 19 us  [the longest x2 15.4 us: swap_chips(): return lax.ppermute(x, 'depth', pairs)]
    ppermute x0 -> x4, starting transfers between devices: none -> 9.29 us  [the longest x2 5.12 us: swap_chips(): return lax.ppermute(x, 'depth', pairs)]
    dot_general x2, matrix products: 9.27 us -> 2.76 us  [the longest x1 1.38 us: shards(): outs = jnp.dot(active, weight_out, preferred_element_type=f32).astype(bf16)]
  transfers between devices with their start and end apart: 3 -> 4, of which waited for: 3 -> 4; matrix products, arithmetic and copies ran while one was open for 0% -> 0% of each run, Pallas kernels for 0% -> 0%
where the time goes in v2:
time: 123 us; the launch traced here: 122 us
  blocking collectives  87.6 us (71%)
  waiting for transfers between devices  19 us (15%)
  starting transfers between devices  9.29 us (8%)
  matrix products  2.76 us (2%)
  other arithmetic  2.1 us (2%)
    all_to_all x1, blocking collectives, shards(): lax.all_to_all(repeat(tokens, members), PLANE, 0, 0, axis_index_groups=far)  32.2 us
    all_to_all x1, blocking collectives, shards(): lax.all_to_all(total.astype(bf16).reshape(members, own, width), PLANE, 0,...  24.7 us
    all_to_all x1, blocking collectives, shards(): lax.all_to_all(repeat(mine, 4), ALL, 0, 0, axis_index_groups=near)  15.5 us
    ppermute x2, waiting for transfers between devices, swap_chips(): return lax.ppermute(x, 'depth', pairs)  15.4 us
    all_to_all x1, blocking collectives, shards(): lax.all_to_all(outs.reshape(4, quarter, width), ALL, 0, 0, axis_index_gro...  15.2 us
    ppermute x2, starting transfers between devices, swap_chips(): return lax.ppermute(x, 'depth', pairs)  5.12 us
    ppermute x2, starting transfers between devices, swap_cores(): lax.ppermute(x, 'depth', [(d, d ^ 1) for d in range(lax.axis_size('depth'...  4.17 us
    ppermute x2, waiting for transfers between devices, swap_cores(): lax.ppermute(x, 'depth', [(d, d ^ 1) for d in range(lax.axis_size('depth'...  3.61 us
  transfers between devices with their start and end apart: 4, of which 4 were waited for; matrix products, arithmetic and copies ran while one was open for 0% of the time, Pallas kernels for 0%

profile of v2, /device:TPU:6, one launch (start us, length us, event | category | flops | bytes accessed | tf_op | source)
XLA Modules:
  0.0 122.0 jit_solution(15170847626353832512)
XLA Ops:
  0.0 0.0 copy-start
  0.0 0.9 broadcast_in_dim.6
  0.9 32.2 %all_to_all.20 = bf16[16,8,1536]{2,1,0:T(8,128)(2,1)S(1)} all-to-all(bf16[16,8,1536]{2,1,0:T(8,128)(2,1)S(1)} %broadcast_in_dim.6), channel_id=1, replica_groups={{0,16,32,48,128,144,160,176,256,272,288,304,384,400,416,432},{8,24,40,5..., dimensions={0} | all-to-all | bytes 786432 | tf_op jit(solution)/shard_map/all_to_all | solution.py:60
  33.2 0.1 broadcast_in_dim.8
  33.3 0.0 copy-start.3
  33.3 15.5 %all_to_all.21 = bf16[4,128,1536]{2,1,0:T(8,128)(2,1)S(1)} all-to-all(bf16[4,128,1536]{2,1,0:T(8,128)(2,1)S(1)} %broadcast_in_dim.8), channel_id=1, replica_groups={{0,8,64,72},{16,24,80,88},{32,40,96,104},{48,56,112,120},{128,136,192,2..., dimensions={0} | all-to-all | bytes 3145728 | tf_op jit(solution)/shard_map/all_to_all | solution.py:61
  48.8 0.0 copy-done.3
  48.8 1.4 %fusion = f32[4,2,64,768]{3,2,1,0:T(8,128)S(1)} fusion(bf16[4,2,64,1536]{3,2,1,0:T(8,128)(2,1)S(1)} %bitcast.39, bf16[1536,768]{1,0:T(8,128)(2,1)S(1)} %copy-done.3), kind=kOutput, calls=%fused_computation.1 | convolution fusion | flops 1207959552 | bytes 5505024 | tf_op jit(solution)/shard_map/dot_general | solution.py:62
  50.2 0.1 select_bitcast_fusion
  50.3 2.2 %collective-permute-start = (f32[4,64,768]{2,1,0:T(8,128)S(1)}, f32[4,64,768]{2,1,0:T(8,128)S(1)}, u32[]{:S(2)}, u32[]{:S(2)}) collective-permute-start(f32[4,64,768]{2,1,0:T(8,128)S(1)} %select_bitcast_fusion), channel_id=1, source_target_pairs={{0,1},{1,0},{2,3},{3,2},{4,5},{5,4},{6,7},{7,6},{8,9},{9,8},{10,11... | collective-permute-start | bytes 2359304 | tf_op jit(solution)/shard_map/ppermute | solution.py:30
  52.5 1.9 %collective-permute-done = f32[4,64,768]{2,1,0:T(8,128)S(1)} collective-permute-done((f32[4,64,768]{2,1,0:T(8,128)S(1)}, f32[4,64,768]{2,1,0:T(8,128)S(1)}, u32[]{:S(2)}, u32[]{:S(2)}) %collective-permute-start) | collective-permute-done | bytes 786464 | tf_op jit(solution)/shard_map/ppermute | solution.py:30
  54.4 0.1 fusion.16
  54.6 0.0 copy-start.2
  54.6 2.7 %collective-permute-start.1 = (bf16[4,64,768]{2,1,0:T(8,128)(2,1)S(1)}, bf16[4,64,768]{2,1,0:T(8,128)(2,1)S(1)}, u32[]{:S(2)}, u32[]{:S(2)}) collective-permute-start(bf16[4,64,768]{2,1,0:T(8,128)(2,1)S(1)} %get-tuple-element.9), channel_id=1, source_target_pairs={{0,2},{1,7},{2,0},{3,5},{4,6},{5,3},{6,4},{7,1},{8,10},{9,15},{10,... | collective-permute-start | bytes 1179656 | tf_op jit(solution)/shard_map/ppermute | solution.py:40
  57.3 6.9 %collective-permute-done.1 = bf16[4,64,768]{2,1,0:T(8,128)(2,1)S(1)} collective-permute-done((bf16[4,64,768]{2,1,0:T(8,128)(2,1)S(1)}, bf16[4,64,768]{2,1,0:T(8,128)(2,1)S(1)}, u32[]{:S(2)}, u32[]{:S(2)}) %collective-permute-start.1) | collective-permute-done | bytes 393248 | tf_op jit(solution)/shard_map/ppermute | solution.py:40
  64.3 0.1 fusion.14
  64.4 2.4 %collective-permute-start.2 = (bf16[4,64,768]{2,1,0:T(8,128)(2,1)S(1)}, bf16[4,64,768]{2,1,0:T(8,128)(2,1)S(1)}, u32[]{:S(2)}, u32[]{:S(2)}) collective-permute-start(bf16[4,64,768]{2,1,0:T(8,128)(2,1)S(1)} %fusion.14), channel_id=1, source_target_pairs={{0,6},{1,3},{2,4},{3,1},{4,2},{5,7},{6,0},{7,5},{8,14},{9,11},{10,... | collective-permute-start | bytes 1179656 | tf_op jit(solution)/shard_map/ppermute | solution.py:40
  66.8 8.5 %collective-permute-done.2 = bf16[4,64,768]{2,1,0:T(8,128)(2,1)S(1)} collective-permute-done((bf16[4,64,768]{2,1,0:T(8,128)(2,1)S(1)}, bf16[4,64,768]{2,1,0:T(8,128)(2,1)S(1)}, u32[]{:S(2)}, u32[]{:S(2)}) %collective-permute-start.2) | collective-permute-done | bytes 393248 | tf_op jit(solution)/shard_map/ppermute | solution.py:40
  75.2 0.0 copy-done.2
  75.2 0.4 fusion.9
  75.6 1.9 %collective-permute-start.3 = (bf16[4,64,768]{2,1,0:T(8,128)(2,1)S(1)}, bf16[4,64,768]{2,1,0:T(8,128)(2,1)S(1)}, u32[]{:S(2)}, u32[]{:S(2)}) collective-permute-start(bf16[4,64,768]{2,1,0:T(8,128)(2,1)S(1)} %fusion.9), channel_id=1, source_target_pairs={{0,1},{1,0},{2,3},{3,2},{4,5},{5,4},{6,7},{7,6},{8,9},{9,8},{10,11... | collective-permute-start | bytes 1179656 | tf_op jit(solution)/shard_map/ppermute | solution.py:30
  77.6 1.7 %collective-permute-done.3 = bf16[4,64,768]{2,1,0:T(8,128)(2,1)S(1)} collective-permute-done((bf16[4,64,768]{2,1,0:T(8,128)(2,1)S(1)}, bf16[4,64,768]{2,1,0:T(8,128)(2,1)S(1)}, u32[]{:S(2)}, u32[]{:S(2)}) %collective-permute-start.3) | collective-permute-done | bytes 393248 | tf_op jit(solution)/shard_map/ppermute | solution.py:30
  79.2 0.1 select_bitcast_fusion.2
  79.3 0.1 pad_maximum_fusion
  79.4 0.1 copy.14
  79.4 0.0 copy-done
  79.5 1.4 %convolution_convert_fusion = bf16[512,1536]{1,0:T(8,128)(2,1)S(1)} fusion(bf16[512,768]{1,0:T(8,128)(2,1)S(1)} %bitcast.42, bf16[768,1536]{1,0:T(8,128)(2,1)S(1)} %copy-done), kind=kOutput, calls=%fused_computation | convolution fusion | flops 1208745984 | bytes 4718592 | tf_op jit(solution)/shard_map/dot_general | solution.py:75
  80.8 15.2 %all_to_all.22 = bf16[4,128,1536]{2,1,0:T(8,128)(2,1)S(1)} all-to-all(bf16[4,128,1536]{2,1,0:T(8,128)(2,1)S(1)} %bitcast.40), channel_id=1, replica_groups={{0,8,64,72},{16,24,80,88},{32,40,96,104},{48,56,112,120},{128,136,192,2..., dimensions={0} | all-to-all | bytes 3145728 | tf_op jit(solution)/shard_map/all_to_all | solution.py:76
  96.0 0.4 convert_element_type.40
  96.4 0.0 copy-start.1
  96.5 0.2 fusion.15
  96.7 24.7 %all_to_all.23 = bf16[16,8,1536]{2,1,0:T(8,128)(2,1)S(1)} all-to-all(bf16[16,8,1536]{2,1,0:T(8,128)(2,1)S(1)} %fusion.15), channel_id=1, replica_groups={{0,16,32,48,128,144,160,176,256,272,288,304,384,400,416,432},{8,24,40,5..., dimensions={0} | all-to-all | bytes 786432 | tf_op jit(solution)/shard_map/all_to_all | solution.py:77
  121.3 0.1 convert_reduce_fusion
  121.4 0.0 copy-done.1
  121.4 0.6 add_convert_fusion
Async XLA Ops:
  0.0 79.5 %copy-start = (bf16[768,1536]{1,0:T(8,128)(2,1)S(1)}, bf16[768,1536]{1,0:T(8,128)(2,1)}, u32[]{:S(2)}) copy-start(bf16[768,1536]{1,0:T(8,128)(2,1)} %param.8) | copy-start | bytes 7077892
  33.3 15.5 %copy-start.3 = (bf16[1536,768]{1,0:T(8,128)(2,1)S(1)}, bf16[1536,768]{1,0:T(8,128)(2,1)}, u32[]{:S(2)}) copy-start(bf16[1536,768]{1,0:T(8,128)(2,1)} %param.6) | copy-start | bytes 7077892
  50.3 4.2 %collective-permute-start = (f32[4,64,768]{2,1,0:T(8,128)S(1)}, f32[4,64,768]{2,1,0:T(8,128)S(1)}, u32[]{:S(2)}, u32[]{:S(2)}) collective-permute-start(f32[4,64,768]{2,1,0:T(8,128)S(1)} %select_bitcast_fusion), channel_id=1, source_target_pairs={{0,1},{1,0},{2,3},{3,2},{4,5},{5,4},{6,7},{7,6},{8,9},{9,8},{10,11... | collective-permute-start | bytes 2359304 | tf_op jit(solution)/shard_map/ppermute | solution.py:30
  54.6 20.7 %copy-start.2 = (f32[768]{0:T(1024)S(1)}, f32[768]{0:T(1024)}, u32[]{:S(2)}) copy-start(f32[768]{0:T(1024)} %param.7) | copy-start | bytes 9220
  54.6 9.7 %collective-permute-start.1 = (bf16[4,64,768]{2,1,0:T(8,128)(2,1)S(1)}, bf16[4,64,768]{2,1,0:T(8,128)(2,1)S(1)}, u32[]{:S(2)}, u32[]{:S(2)}) collective-permute-start(bf16[4,64,768]{2,1,0:T(8,128)(2,1)S(1)} %get-tuple-element.9), channel_id=1, source_target_pairs={{0,2},{1,7},{2,0},{3,5},{4,6},{5,3},{6,4},{7,1},{8,10},{9,15},{10,... | collective-permute-start | bytes 1179656 | tf_op jit(solution)/shard_map/ppermute | solution.py:40
  64.4 10.9 %collective-permute-start.2 = (bf16[4,64,768]{2,1,0:T(8,128)(2,1)S(1)}, bf16[4,64,768]{2,1,0:T(8,128)(2,1)S(1)}, u32[]{:S(2)}, u32[]{:S(2)}) collective-permute-start(bf16[4,64,768]{2,1,0:T(8,128)(2,1)S(1)} %fusion.14), channel_id=1, source_target_pairs={{0,6},{1,3},{2,4},{3,1},{4,2},{5,7},{6,0},{7,5},{8,14},{9,11},{10,... | collective-permute-start | bytes 1179656 | tf_op jit(solution)/shard_map/ppermute | solution.py:40
  75.6 3.6 %collective-permute-start.3 = (bf16[4,64,768]{2,1,0:T(8,128)(2,1)S(1)}, bf16[4,64,768]{2,1,0:T(8,128)(2,1)S(1)}, u32[]{:S(2)}, u32[]{:S(2)}) collective-permute-start(bf16[4,64,768]{2,1,0:T(8,128)(2,1)S(1)} %fusion.9), channel_id=1, source_target_pairs={{0,1},{1,0},{2,3},{3,2},{4,5},{5,4},{6,7},{7,6},{8,9},{9,8},{10,11... | collective-permute-start | bytes 1179656 | tf_op jit(solution)/shard_map/ppermute | solution.py:30
  96.4 24.9 %copy-start.1 = (f32[1536]{0:T(1024)S(1)}, f32[1536]{0:T(1024)}, u32[]{:S(2)}) copy-start(f32[1536]{0:T(1024)} %param.9) | copy-start | bytes 18436

commit v3 on v2

v3 whole, which is shorter than its diff:
```python
import jax
import jax.numpy as jnp
from jax import lax
from jax.sharding import PartitionSpec as P

ALL = ("rows", "cols", "depth")


def parity_groups(n_rows, n_cols, n_depth):
    groups = []
    for d in range(n_depth):
        for p in range(2):
            for q in range(2):
                chips = [r * n_cols + c for r in range(p, n_rows, 2) for c in range(q, n_cols, 2)]
                half = len(chips) // 2 * (d % 2)
                groups.append([chip * n_depth + d for chip in chips[half:] + chips[:half]])
    return groups


def square_groups(n_rows, n_cols, n_depth):
    groups = []
    for d in range(n_depth):
        for r in range(d % 2, n_rows + d % 2, 2):
            for c in range(1 - d % 2, n_cols + 1 - d % 2, 2):
                chips = [(i % n_rows, j % n_cols) for i in (r, r + 1) for j in (c, c + 1)]
                chips.sort(key=lambda chip: (chip[0] % 2, chip[1] % 2))
                groups.append([(i * n_cols + j) * n_depth + d for i, j in chips])
    return groups


def swap_cores(x):
    return lax.ppermute(x, "depth", [(d, d ^ 1) for d in range(lax.axis_size("depth"))])


def swap_chips(x, stage):
    n = lax.axis_size("depth")
    pairs = []
    for d in range(n):
        chip, core = d // 2, d % 2
        step = 1 if (chip + core + stage) % 2 == 0 else -1
        pairs.append((d, ((chip + step) * 2 + core) % n))
    return lax.ppermute(x, "depth", pairs)


def shards(tokens, weight_in, bias_in, weight_out, bias_out):
    own, width = tokens.shape
    n_rows, n_cols, n_depth = (lax.axis_size(a) for a in ALL)
    far, near = parity_groups(n_rows, n_cols, n_depth), square_groups(n_rows, n_cols, n_depth)
    members = n_rows * n_cols // 4
    quarter = members * own
    f32, bf16 = jnp.float32, jnp.bfloat16

    def repeat(x, n):
        return jnp.broadcast_to(x[None], (n,) + x.shape)

    def add(x):
        x = x.astype(f32)
        return (x[0] + x[1]) + (x[2] + x[3])

    mine = lax.all_to_all(repeat(tokens, members), ALL, 0, 0, axis_index_groups=far).reshape(quarter, width)
    full = lax.all_to_all(repeat(mine, 4), ALL, 0, 0, axis_index_groups=near).reshape(-1, width)
    partial = jnp.dot(full, weight_in, preferred_element_type=f32)

    ours, theirs = jnp.unstack(partial.reshape(4, 2, quarter // 2, -1), axis=1)
    ours = ours + swap_cores(theirs)
    for stage in range(2):
        ours = ours + swap_chips(ours.astype(bf16), stage).astype(f32)
    ours = jax.nn.gelu(ours + bias_in, approximate=True).astype(bf16)
    active = jnp.stack([ours, swap_cores(ours)], axis=1).reshape(4 * quarter, -1)

    outs = jnp.dot(active, weight_out, preferred_element_type=f32).astype(bf16)
    total = add(lax.all_to_all(outs.reshape(4, quarter, width), ALL, 0, 0, axis_index_groups=near))
    parts = lax.all_to_all(total.astype(bf16).reshape(members, own, width), ALL, 0, 0, axis_index_groups=far)
    return (jnp.sum(parts.astype(f32), axis=0) + bias_out).astype(bf16)


def solution(mesh):
    in_specs = (
        P(("rows", "cols"), "depth"),
        P("depth", ("rows", "cols")),
        P(("rows", "cols")),
        P(("rows", "cols"), "depth"),
        P("depth"),
    )
    out_specs = P(("rows", "cols"), "depth")
    return jax.shard_map(shards, mesh=mesh, in_specs=in_specs, out_specs=out_specs, check_vma=False)
```

time: 123 us -> 122 us (level)
    all_to_all x2, blocking collectives: 56.9 us -> 53.9 us  [the longest x1 31.1 us: shards(): lax.all_to_all(repeat(tokens, members), ALL, 0, 0, axis_index_groups=far)]
where the time goes in v3:
time: 122 us; the launch traced here: 121 us
  blocking collectives  86.9 us (71%)
  waiting for transfers between devices  19.4 us (16%)
  starting transfers between devices  8.96 us (7%)
  matrix products  2.76 us (2%)
  other arithmetic  2 us (2%)
    all_to_all x1, blocking collectives, shards(): lax.all_to_all(repeat(tokens, members), ALL, 0, 0, axis_index_groups=far)  31.1 us
    all_to_all x1, blocking collectives, shards(): lax.all_to_all(total.astype(bf16).reshape(members, own, width), ALL, 0, 0...  22.8 us
    all_to_all x1, blocking collectives, shards(): lax.all_to_all(repeat(mine, 4), ALL, 0, 0, axis_index_groups=near)  16.7 us
    all_to_all x1, blocking collectives, shards(): lax.all_to_all(outs.reshape(4, quarter, width), ALL, 0, 0, axis_index_gro...  16.4 us
    ppermute x2, waiting for transfers between devices, swap_chips(): return lax.ppermute(x, 'depth', pairs)  15.4 us
    ppermute x2, starting transfers between devices, swap_chips(): return lax.ppermute(x, 'depth', pairs)  5.12 us
    ppermute x2, waiting for transfers between devices, swap_cores(): lax.ppermute(x, 'depth', [(d, d ^ 1) for d in range(lax.axis_size('depth'...  3.94 us
    ppermute x2, starting transfers between devices, swap_cores(): lax.ppermute(x, 'depth', [(d, d ^ 1) for d in range(lax.axis_size('depth'...  3.84 us
  transfers between devices with their start and end apart: 4, of which 4 were waited for; matrix products, arithmetic and copies ran while one was open for 0% of the time, Pallas kernels for 0%

profile of v3, /device:TPU:6, one launch (start us, length us, event | category | flops | bytes accessed | tf_op | source)
XLA Modules:
  0.0 121.3 jit_solution(14205007992664709610)
XLA Ops:
  0.0 0.0 copy-start
  0.0 0.9 broadcast_in_dim.6
  0.9 31.1 %all_to_all.20 = bf16[16,8,1536]{2,1,0:T(8,128)(2,1)S(1)} all-to-all(bf16[16,8,1536]{2,1,0:T(8,128)(2,1)S(1)} %broadcast_in_dim.6), channel_id=1, replica_groups={{0,16,32,48,128,144,160,176,256,272,288,304,384,400,416,432},{8,24,40,5..., dimensions={0} | all-to-all | bytes 786432 | tf_op jit(solution)/shard_map/all_to_all | solution.py:60
  32.0 0.1 broadcast_in_dim.8
  32.1 0.0 copy-start.3
  32.1 16.7 %all_to_all.21 = bf16[4,128,1536]{2,1,0:T(8,128)(2,1)S(1)} all-to-all(bf16[4,128,1536]{2,1,0:T(8,128)(2,1)S(1)} %broadcast_in_dim.8), channel_id=1, replica_groups={{16,8,80,72},{32,24,96,88},{48,40,112,104},{0,56,64,120},{144,136,208,2..., dimensions={0} | all-to-all | bytes 3145728 | tf_op jit(solution)/shard_map/all_to_all | solution.py:61
  48.8 0.0 copy-done.3
  48.8 1.4 %fusion = f32[4,2,64,768]{3,2,1,0:T(8,128)S(1)} fusion(bf16[4,2,64,1536]{3,2,1,0:T(8,128)(2,1)S(1)} %bitcast.30, bf16[1536,768]{1,0:T(8,128)(2,1)S(1)} %copy-done.3), kind=kOutput, calls=%fused_computation.1 | convolution fusion | flops 1207959552 | bytes 5505024 | tf_op jit(solution)/shard_map/dot_general | solution.py:62
  50.2 0.1 slice_bitcast_fusion
  50.2 1.9 %collective-permute-start = (f32[4,64,768]{2,1,0:T(8,128)S(1)}, f32[4,64,768]{2,1,0:T(8,128)S(1)}, u32[]{:S(2)}, u32[]{:S(2)}) collective-permute-start(f32[4,64,768]{2,1,0:T(8,128)S(1)} %slice_bitcast_fusion), channel_id=1, source_target_pairs={{0,1},{1,0},{2,3},{3,2},{4,5},{5,4},{6,7},{7,6},{8,9},{9,8},{10,11... | collective-permute-start | bytes 2359304 | tf_op jit(solution)/shard_map/ppermute | solution.py:32
  52.2 2.3 %collective-permute-done = f32[4,64,768]{2,1,0:T(8,128)S(1)} collective-permute-done((f32[4,64,768]{2,1,0:T(8,128)S(1)}, f32[4,64,768]{2,1,0:T(8,128)S(1)}, u32[]{:S(2)}, u32[]{:S(2)}) %collective-permute-start) | collective-permute-done | bytes 786464 | tf_op jit(solution)/shard_map/ppermute | solution.py:32
  54.4 0.1 fusion.15
  54.5 0.0 copy-start.2
  54.5 2.7 %collective-permute-start.1 = (bf16[4,64,768]{2,1,0:T(8,128)(2,1)S(1)}, bf16[4,64,768]{2,1,0:T(8,128)(2,1)S(1)}, u32[]{:S(2)}, u32[]{:S(2)}) collective-permute-start(bf16[4,64,768]{2,1,0:T(8,128)(2,1)S(1)} %fusion.15), channel_id=1, source_target_pairs={{0,2},{1,7},{2,0},{3,5},{4,6},{5,3},{6,4},{7,1},{8,10},{9,15},{10,... | collective-permute-start | bytes 1179656 | tf_op jit(solution)/shard_map/ppermute | solution.py:42
  57.3 6.9 %collective-permute-done.1 = bf16[4,64,768]{2,1,0:T(8,128)(2,1)S(1)} collective-permute-done((bf16[4,64,768]{2,1,0:T(8,128)(2,1)S(1)}, bf16[4,64,768]{2,1,0:T(8,128)(2,1)S(1)}, u32[]{:S(2)}, u32[]{:S(2)}) %collective-permute-start.1) | collective-permute-done | bytes 393248 | tf_op jit(solution)/shard_map/ppermute | solution.py:42
  64.2 0.1 fusion.13
  64.4 2.4 %collective-permute-start.2 = (bf16[4,64,768]{2,1,0:T(8,128)(2,1)S(1)}, bf16[4,64,768]{2,1,0:T(8,128)(2,1)S(1)}, u32[]{:S(2)}, u32[]{:S(2)}) collective-permute-start(bf16[4,64,768]{2,1,0:T(8,128)(2,1)S(1)} %fusion.13), channel_id=1, source_target_pairs={{0,6},{1,3},{2,4},{3,1},{4,2},{5,7},{6,0},{7,5},{8,14},{9,11},{10,... | collective-permute-start | bytes 1179656 | tf_op jit(solution)/shard_map/ppermute | solution.py:42
  66.8 8.5 %collective-permute-done.2 = bf16[4,64,768]{2,1,0:T(8,128)(2,1)S(1)} collective-permute-done((bf16[4,64,768]{2,1,0:T(8,128)(2,1)S(1)}, bf16[4,64,768]{2,1,0:T(8,128)(2,1)S(1)}, u32[]{:S(2)}, u32[]{:S(2)}) %collective-permute-start.2) | collective-permute-done | bytes 393248 | tf_op jit(solution)/shard_map/ppermute | solution.py:42
  75.2 0.0 copy-done.2
  75.2 0.4 fusion.9
  75.7 1.9 %collective-permute-start.3 = (bf16[4,64,768]{2,1,0:T(8,128)(2,1)S(1)}, bf16[4,64,768]{2,1,0:T(8,128)(2,1)S(1)}, u32[]{:S(2)}, u32[]{:S(2)}) collective-permute-start(bf16[4,64,768]{2,1,0:T(8,128)(2,1)S(1)} %fusion.9), channel_id=1, source_target_pairs={{0,1},{1,0},{2,3},{3,2},{4,5},{5,4},{6,7},{7,6},{8,9},{9,8},{10,11... | collective-permute-start | bytes 1179656 | tf_op jit(solution)/shard_map/ppermute | solution.py:32
  77.6 1.7 %collective-permute-done.3 = bf16[4,64,768]{2,1,0:T(8,128)(2,1)S(1)} collective-permute-done((bf16[4,64,768]{2,1,0:T(8,128)(2,1)S(1)}, bf16[4,64,768]{2,1,0:T(8,128)(2,1)S(1)}, u32[]{:S(2)}, u32[]{:S(2)}) %collective-permute-start.3) | collective-permute-done | bytes 393248 | tf_op jit(solution)/shard_map/ppermute | solution.py:32
  79.3 0.1 pad_maximum_fusion
  79.4 0.1 copy.8
  79.4 0.0 copy-done
  79.4 1.4 %convolution_convert_fusion = bf16[512,1536]{1,0:T(8,128)(2,1)S(1)} fusion(bf16[512,768]{1,0:T(8,128)(2,1)S(1)} %bitcast.34, bf16[768,1536]{1,0:T(8,128)(2,1)S(1)} %copy-done), kind=kOutput, calls=%fused_computation | convolution fusion | flops 1208745984 | bytes 4718592 | tf_op jit(solution)/shard_map/dot_general | solution.py:71
  80.8 16.4 %all_to_all.22 = bf16[4,128,1536]{2,1,0:T(8,128)(2,1)S(1)} all-to-all(bf16[4,128,1536]{2,1,0:T(8,128)(2,1)S(1)} %bitcast.31), channel_id=1, replica_groups={{16,8,80,72},{32,24,96,88},{48,40,112,104},{0,56,64,120},{144,136,208,2..., dimensions={0} | all-to-all | bytes 3145728 | tf_op jit(solution)/shard_map/all_to_all | solution.py:72
  97.2 0.4 convert_element_type.40
  97.6 0.0 copy-start.1
  97.6 0.2 fusion.14
  97.8 22.8 %all_to_all.23 = bf16[16,8,1536]{2,1,0:T(8,128)(2,1)S(1)} all-to-all(bf16[16,8,1536]{2,1,0:T(8,128)(2,1)S(1)} %fusion.14), channel_id=1, replica_groups={{0,16,32,48,128,144,160,176,256,272,288,304,384,400,416,432},{8,24,40,5..., dimensions={0} | all-to-all | bytes 786432 | tf_op jit(solution)/shard_map/all_to_all | solution.py:73
  120.6 0.1 convert_reduce_fusion
  120.7 0.0 copy-done.1
  120.7 0.6 add_convert_fusion
Async XLA Ops:
  0.0 79.4 %copy-start = (bf16[768,1536]{1,0:T(8,128)(2,1)S(1)}, bf16[768,1536]{1,0:T(8,128)(2,1)}, u32[]{:S(2)}) copy-start(bf16[768,1536]{1,0:T(8,128)(2,1)} %param.8) | copy-start | bytes 7077892
  32.1 16.7 %copy-start.3 = (bf16[1536,768]{1,0:T(8,128)(2,1)S(1)}, bf16[1536,768]{1,0:T(8,128)(2,1)}, u32[]{:S(2)}) copy-start(bf16[1536,768]{1,0:T(8,128)(2,1)} %param.6) | copy-start | bytes 7077892
  50.2 4.2 %collective-permute-start = (f32[4,64,768]{2,1,0:T(8,128)S(1)}, f32[4,64,768]{2,1,0:T(8,128)S(1)}, u32[]{:S(2)}, u32[]{:S(2)}) collective-permute-start(f32[4,64,768]{2,1,0:T(8,128)S(1)} %slice_bitcast_fusion), channel_id=1, source_target_pairs={{0,1},{1,0},{2,3},{3,2},{4,5},{5,4},{6,7},{7,6},{8,9},{9,8},{10,11... | collective-permute-start | bytes 2359304 | tf_op jit(solution)/shard_map/ppermute | solution.py:32
  54.5 20.7 %copy-start.2 = (f32[768]{0:T(1024)S(1)}, f32[768]{0:T(1024)}, u32[]{:S(2)}) copy-start(f32[768]{0:T(1024)} %param.7) | copy-start | bytes 9220
  54.5 9.7 %collective-permute-start.1 = (bf16[4,64,768]{2,1,0:T(8,128)(2,1)S(1)}, bf16[4,64,768]{2,1,0:T(8,128)(2,1)S(1)}, u32[]{:S(2)}, u32[]{:S(2)}) collective-permute-start(bf16[4,64,768]{2,1,0:T(8,128)(2,1)S(1)} %fusion.15), channel_id=1, source_target_pairs={{0,2},{1,7},{2,0},{3,5},{4,6},{5,3},{6,4},{7,1},{8,10},{9,15},{10,... | collective-permute-start | bytes 1179656 | tf_op jit(solution)/shard_map/ppermute | solution.py:42
  64.4 10.9 %collective-permute-start.2 = (bf16[4,64,768]{2,1,0:T(8,128)(2,1)S(1)}, bf16[4,64,768]{2,1,0:T(8,128)(2,1)S(1)}, u32[]{:S(2)}, u32[]{:S(2)}) collective-permute-start(bf16[4,64,768]{2,1,0:T(8,128)(2,1)S(1)} %fusion.13), channel_id=1, source_target_pairs={{0,6},{1,3},{2,4},{3,1},{4,2},{5,7},{6,0},{7,5},{8,14},{9,11},{10,... | collective-permute-start | bytes 1179656 | tf_op jit(solution)/shard_map/ppermute | solution.py:42
  75.7 3.6 %collective-permute-start.3 = (bf16[4,64,768]{2,1,0:T(8,128)(2,1)S(1)}, bf16[4,64,768]{2,1,0:T(8,128)(2,1)S(1)}, u32[]{:S(2)}, u32[]{:S(2)}) collective-permute-start(bf16[4,64,768]{2,1,0:T(8,128)(2,1)S(1)} %fusion.9), channel_id=1, source_target_pairs={{0,1},{1,0},{2,3},{3,2},{4,5},{5,4},{6,7},{7,6},{8,9},{9,8},{10,11... | collective-permute-start | bytes 1179656 | tf_op jit(solution)/shard_map/ppermute | solution.py:32
  97.6 23.1 %copy-start.1 = (f32[1536]{0:T(1024)S(1)}, f32[1536]{0:T(1024)}, u32[]{:S(2)}) copy-start(f32[1536]{0:T(1024)} %param.9) | copy-start | bytes 18436

commit v4 on v3

--- a/solution.py
+++ b/solution.py
@@ -59,16 +59,19 @@
 
     mine = lax.all_to_all(repeat(tokens, members), ALL, 0, 0, axis_index_groups=far).reshape(quarter, width)
     full = lax.all_to_all(repeat(mine, 4), ALL, 0, 0, axis_index_groups=near).reshape(-1, width)
-    partial = jnp.dot(full, weight_in, preferred_element_type=f32)
 
-    ours, theirs = jnp.unstack(partial.reshape(4, 2, quarter // 2, -1), axis=1)
-    ours = ours + swap_cores(theirs)
+    ours, theirs = jnp.unstack(full.reshape(4, 2, quarter // 2, width), axis=1)
+    theirs = swap_cores(jnp.dot(theirs, weight_in, preferred_element_type=f32))
+    ours = jnp.dot(ours, weight_in, preferred_element_type=f32)
+    ours, theirs = lax.optimization_barrier((ours, theirs))
+    ours = ours + theirs
     for stage in range(2):
         ours = ours + swap_chips(ours.astype(bf16), stage).astype(f32)
     ours = jax.nn.gelu(ours + bias_in, approximate=True).astype(bf16)
-    active = jnp.stack([ours, swap_cores(ours)], axis=1).reshape(4 * quarter, -1)
+    active = [ours, swap_cores(ours)]
 
-    outs = jnp.dot(active, weight_out, preferred_element_type=f32).astype(bf16)
+    outs = [jnp.dot(a, weight_out, preferred_element_type=f32).astype(bf16) for a in active]
+    outs = jnp.stack(outs, axis=1)
     total = add(lax.all_to_all(outs.reshape(4, quarter, width), ALL, 0, 0, axis_index_groups=near))
     parts = lax.all_to_all(total.astype(bf16).reshape(members, own, width), ALL, 0, 0, axis_index_groups=far)
     return (jnp.sum(parts.astype(f32), axis=0) + bias_out).astype(bf16)

time: 122 us -> 120 us (0.984)
  waiting for transfers between devices: 19.4 us -> 17.8 us
    ppermute x2, waiting for transfers between devices: 3.94 us -> 2.36 us  [swap_cores(): lax.ppermute(x, 'depth', [(d, d ^ 1) for d in range(lax.axis_size('depth'...]
    dot_general x2 -> x4, matrix products: 2.76 us -> 3.09 us  [the longest x2 1.54 us: shards(): jnp.dot(a, weight_out, preferred_element_type=f32).astype(bf16)]
  transfers between devices with their start and end apart: 4 -> 4, of which waited for: 4 -> 4; matrix products, arithmetic and copies ran while one was open for 0% -> 1% of each run, Pallas kernels for 0% -> 0%
where the time goes in v4:
time: 120 us
  blocking collectives  86.9 us (72%)
  waiting for transfers between devices  17.8 us (15%)
  starting transfers between devices  8.96 us (7%)
  matrix products  3.09 us (3%)
  other arithmetic  1.96 us (2%)
    all_to_all x1, blocking collectives, shards(): lax.all_to_all(repeat(tokens, members), ALL, 0, 0, axis_index_groups=far)  31.1 us
    all_to_all x1, blocking collectives, shards(): lax.all_to_all(total.astype(bf16).reshape(members, own, width), ALL, 0, 0...  22.8 us
    all_to_all x1, blocking collectives, shards(): lax.all_to_all(repeat(mine, 4), ALL, 0, 0, axis_index_groups=near)  16.7 us
    all_to_all x1, blocking collectives, shards(): lax.all_to_all(outs.reshape(4, quarter, width), ALL, 0, 0, axis_index_gro...  16.4 us
    ppermute x2, waiting for transfers between devices, swap_chips(): return lax.ppermute(x, 'depth', pairs)  15.4 us
    ppermute x2, starting transfers between devices, swap_chips(): return lax.ppermute(x, 'depth', pairs)  5.12 us
    ppermute x2, starting transfers between devices, swap_cores(): lax.ppermute(x, 'depth', [(d, d ^ 1) for d in range(lax.axis_size('depth'...  3.84 us
  transfers between devices with their start and end apart: 4, of which 4 were waited for; matrix products, arithmetic and copies ran while one was open for 1% of the time, Pallas kernels for 0%

profile of v4, /device:TPU:6, one launch (start us, length us, event | category | flops | bytes accessed | tf_op | source)
XLA Modules:
  0.0 120.0 jit_solution(6503744124385093627)
XLA Ops:
  0.0 0.0 copy-start
  0.0 0.9 broadcast_in_dim.6
  0.9 31.1 %all_to_all.20 = bf16[16,8,1536]{2,1,0:T(8,128)(2,1)S(1)} all-to-all(bf16[16,8,1536]{2,1,0:T(8,128)(2,1)S(1)} %broadcast_in_dim.6), channel_id=1, replica_groups={{0,16,32,48,128,144,160,176,256,272,288,304,384,400,416,432},{8,24,40,5..., dimensions={0} | all-to-all | bytes 786432 | tf_op jit(solution)/shard_map/all_to_all | solution.py:60
  32.0 0.0 copy-start.3
  32.0 0.1 broadcast_in_dim.8
  32.1 16.7 %all_to_all.21 = bf16[4,128,1536]{2,1,0:T(8,128)(2,1)S(1)} all-to-all(bf16[4,128,1536]{2,1,0:T(8,128)(2,1)S(1)} %broadcast_in_dim.8), channel_id=1, replica_groups={{16,8,80,72},{32,24,96,88},{48,40,112,104},{0,56,64,120},{144,136,208,2..., dimensions={0} | all-to-all | bytes 3145728 | tf_op jit(solution)/shard_map/all_to_all | solution.py:61
  48.8 0.0 copy-done.3
  48.8 0.8 fusion.4
  49.6 1.9 %collective-permute-start = (f32[4,64,768]{2,1,0:T(8,128)S(1)}, f32[4,64,768]{2,1,0:T(8,128)S(1)}, u32[]{:S(2)}, u32[]{:S(2)}) collective-permute-start(f32[4,64,768]{2,1,0:T(8,128)S(1)} %fusion.4), channel_id=1, source_target_pairs={{0,1},{1,0},{2,3},{3,2},{4,5},{5,4},{6,7},{7,6},{8,9},{9,8},{10,11... | collective-permute-start | bytes 2359304 | tf_op jit(solution)/shard_map/ppermute | solution.py:32
  51.5 0.8 fusion.6
  52.3 0.0 copy-start.2
  52.3 1.5 %collective-permute-done = f32[4,64,768]{2,1,0:T(8,128)S(1)} collective-permute-done((f32[4,64,768]{2,1,0:T(8,128)S(1)}, f32[4,64,768]{2,1,0:T(8,128)S(1)}, u32[]{:S(2)}, u32[]{:S(2)}) %collective-permute-start) | collective-permute-done | bytes 786464 | tf_op jit(solution)/shard_map/ppermute | solution.py:32
  53.7 0.1 fusion.20
  53.9 2.7 %collective-permute-start.1 = (bf16[4,64,768]{2,1,0:T(8,128)(2,1)S(1)}, bf16[4,64,768]{2,1,0:T(8,128)(2,1)S(1)}, u32[]{:S(2)}, u32[]{:S(2)}) collective-permute-start(bf16[4,64,768]{2,1,0:T(8,128)(2,1)S(1)} %get-tuple-element.9), channel_id=1, source_target_pairs={{0,2},{1,7},{2,0},{3,5},{4,6},{5,3},{6,4},{7,1},{8,10},{9,15},{10,... | collective-permute-start | bytes 1179656 | tf_op jit(solution)/shard_map/ppermute | solution.py:42
  56.6 6.9 %collective-permute-done.1 = bf16[4,64,768]{2,1,0:T(8,128)(2,1)S(1)} collective-permute-done((bf16[4,64,768]{2,1,0:T(8,128)(2,1)S(1)}, bf16[4,64,768]{2,1,0:T(8,128)(2,1)S(1)}, u32[]{:S(2)}, u32[]{:S(2)}) %collective-permute-start.1) | collective-permute-done | bytes 393248 | tf_op jit(solution)/shard_map/ppermute | solution.py:42
  63.5 0.1 fusion.18
  63.6 2.4 %collective-permute-start.2 = (bf16[4,64,768]{2,1,0:T(8,128)(2,1)S(1)}, bf16[4,64,768]{2,1,0:T(8,128)(2,1)S(1)}, u32[]{:S(2)}, u32[]{:S(2)}) collective-permute-start(bf16[4,64,768]{2,1,0:T(8,128)(2,1)S(1)} %fusion.18), channel_id=1, source_target_pairs={{0,6},{1,3},{2,4},{3,1},{4,2},{5,7},{6,0},{7,5},{8,14},{9,11},{10,... | collective-permute-start | bytes 1179656 | tf_op jit(solution)/shard_map/ppermute | solution.py:42
  66.0 8.5 %collective-permute-done.2 = bf16[4,64,768]{2,1,0:T(8,128)(2,1)S(1)} collective-permute-done((bf16[4,64,768]{2,1,0:T(8,128)(2,1)S(1)}, bf16[4,64,768]{2,1,0:T(8,128)(2,1)S(1)}, u32[]{:S(2)}, u32[]{:S(2)}) %collective-permute-start.2) | collective-permute-done | bytes 393248 | tf_op jit(solution)/shard_map/ppermute | solution.py:42
  74.5 0.0 copy-done.2
  74.5 0.4 fusion.15
  74.9 1.9 %collective-permute-start.3 = (bf16[4,64,768]{2,1,0:T(8,128)(2,1)S(1)}, bf16[4,64,768]{2,1,0:T(8,128)(2,1)S(1)}, u32[]{:S(2)}, u32[]{:S(2)}) collective-permute-start(bf16[4,64,768]{2,1,0:T(8,128)(2,1)S(1)} %fusion.15), channel_id=1, source_target_pairs={{0,1},{1,0},{2,3},{3,2},{4,5},{5,4},{6,7},{7,6},{8,9},{9,8},{10,11... | collective-permute-start | bytes 1179656 | tf_op jit(solution)/shard_map/ppermute | solution.py:32
  76.8 0.0 copy-done
  76.8 0.8 fusion
  77.6 0.9 collective-permute-done.3
  78.5 0.8 fusion.1
  79.3 0.1 pad_maximum_fusion
  79.4 0.1 copy.8
  79.5 16.4 %all_to_all.22 = bf16[4,128,1536]{2,1,0:T(8,128)(2,1)S(1)} all-to-all(bf16[4,128,1536]{2,1,0:T(8,128)(2,1)S(1)} %bitcast.31), channel_id=1, replica_groups={{16,8,80,72},{32,24,96,88},{48,40,112,104},{0,56,64,120},{144,136,208,2..., dimensions={0} | all-to-all | bytes 3145728 | tf_op jit(solution)/shard_map/all_to_all | solution.py:75
  95.9 0.4 convert_element_type.44
  96.3 0.0 copy-start.1
  96.3 0.2 fusion.19
  96.5 22.8 %all_to_all.23 = bf16[16,8,1536]{2,1,0:T(8,128)(2,1)S(1)} all-to-all(bf16[16,8,1536]{2,1,0:T(8,128)(2,1)S(1)} %fusion.19), channel_id=1, replica_groups={{0,16,32,48,128,144,160,176,256,272,288,304,384,400,416,432},{8,24,40,5..., dimensions={0} | all-to-all | bytes 786432 | tf_op jit(solution)/shard_map/all_to_all | solution.py:76
  119.3 0.1 convert_reduce_fusion
  119.4 0.0 copy-done.1
  119.4 0.6 add_convert_fusion
Async XLA Ops:
  0.0 76.8 %copy-start = (bf16[768,1536]{1,0:T(8,128)(2,1)S(1)}, bf16[768,1536]{1,0:T(8,128)(2,1)}, u32[]{:S(2)}) copy-start(bf16[768,1536]{1,0:T(8,128)(2,1)} %param.8) | copy-start | bytes 7077892
  32.0 16.8 %copy-start.3 = (bf16[1536,768]{1,0:T(8,128)(2,1)S(1)}, bf16[1536,768]{1,0:T(8,128)(2,1)}, u32[]{:S(2)}) copy-start(bf16[1536,768]{1,0:T(8,128)(2,1)} %param.6) | copy-start | bytes 7077892
  49.6 4.2 %collective-permute-start = (f32[4,64,768]{2,1,0:T(8,128)S(1)}, f32[4,64,768]{2,1,0:T(8,128)S(1)}, u32[]{:S(2)}, u32[]{:S(2)}) collective-permute-start(f32[4,64,768]{2,1,0:T(8,128)S(1)} %fusion.4), channel_id=1, source_target_pairs={{0,1},{1,0},{2,3},{3,2},{4,5},{5,4},{6,7},{7,6},{8,9},{9,8},{10,11... | collective-permute-start | bytes 2359304 | tf_op jit(solution)/shard_map/ppermute | solution.py:32
  52.3 22.2 %copy-start.2 = (f32[768]{0:T(1024)S(1)}, f32[768]{0:T(1024)}, u32[]{:S(2)}) copy-start(f32[768]{0:T(1024)} %param.7) | copy-start | bytes 9220
  53.9 9.7 %collective-permute-start.1 = (bf16[4,64,768]{2,1,0:T(8,128)(2,1)S(1)}, bf16[4,64,768]{2,1,0:T(8,128)(2,1)S(1)}, u32[]{:S(2)}, u32[]{:S(2)}) collective-permute-start(bf16[4,64,768]{2,1,0:T(8,128)(2,1)S(1)} %get-tuple-element.9), channel_id=1, source_target_pairs={{0,2},{1,7},{2,0},{3,5},{4,6},{5,3},{6,4},{7,1},{8,10},{9,15},{10,... | collective-permute-start | bytes 1179656 | tf_op jit(solution)/shard_map/ppermute | solution.py:42
  63.6 10.9 %collective-permute-start.2 = (bf16[4,64,768]{2,1,0:T(8,128)(2,1)S(1)}, bf16[4,64,768]{2,1,0:T(8,128)(2,1)S(1)}, u32[]{:S(2)}, u32[]{:S(2)}) collective-permute-start(bf16[4,64,768]{2,1,0:T(8,128)(2,1)S(1)} %fusion.18), channel_id=1, source_target_pairs={{0,6},{1,3},{2,4},{3,1},{4,2},{5,7},{6,0},{7,5},{8,14},{9,11},{10,... | collective-permute-start | bytes 1179656 | tf_op jit(solution)/shard_map/ppermute | solution.py:42
  74.9 3.6 %collective-permute-start.3 = (bf16[4,64,768]{2,1,0:T(8,128)(2,1)S(1)}, bf16[4,64,768]{2,1,0:T(8,128)(2,1)S(1)}, u32[]{:S(2)}, u32[]{:S(2)}) collective-permute-start(bf16[4,64,768]{2,1,0:T(8,128)(2,1)S(1)} %fusion.15), channel_id=1, source_target_pairs={{0,1},{1,0},{2,3},{3,2},{4,5},{5,4},{6,7},{7,6},{8,9},{9,8},{10,11... | collective-permute-start | bytes 1179656 | tf_op jit(solution)/shard_map/ppermute | solution.py:32
  96.3 23.1 %copy-start.1 = (f32[1536]{0:T(1024)S(1)}, f32[1536]{0:T(1024)}, u32[]{:S(2)}) copy-start(f32[1536]{0:T(1024)} %param.9) | copy-start | bytes 18436

commit v5 on v4

--- a/solution.py
+++ b/solution.py
@@ -12,6 +12,7 @@
         for p in range(2):
             for q in range(2):
                 chips = [r * n_cols + c for r in range(p, n_rows, 2) for c in range(q, n_cols, 2)]
+                chips[len(chips) // 2 :] = chips[: len(chips) // 2 - 1 : -1]
                 half = len(chips) // 2 * (d % 2)
                 groups.append([chip * n_depth + d for chip in chips[half:] + chips[:half]])
     return groups
@@ -23,7 +24,7 @@
         for r in range(d % 2, n_rows + d % 2, 2):
             for c in range(1 - d % 2, n_cols + 1 - d % 2, 2):
                 chips = [(i % n_rows, j % n_cols) for i in (r, r + 1) for j in (c, c + 1)]
-                chips.sort(key=lambda chip: (chip[0] % 2, chip[1] % 2))
+                chips.sort(key=lambda chip: ((chip[0] + chip[1]) % 2, chip[0] % 2))
                 groups.append([(i * n_cols + j) * n_depth + d for i, j in chips])
     return groups
 

time: 120 us -> 117 us (0.975)
  blocking collectives: 86.9 us -> 83.5 us
    all_to_all x1, blocking collectives: 22.8 us -> 21.1 us  [shards(): lax.all_to_all(total.astype(bf16).reshape(members, own, width), ALL, 0, 0...]
    all_to_all x1, blocking collectives: 31.1 us -> 29.4 us  [shards(): lax.all_to_all(repeat(tokens, members), ALL, 0, 0, axis_index_groups=far)]
where the time goes in v5:
time: 117 us
  blocking collectives  83.5 us (71%)
  waiting for transfers between devices  17.8 us (15%)
  starting transfers between devices  8.96 us (8%)
  matrix products  3.09 us (3%)
  other arithmetic  1.96 us (2%)
    all_to_all x1, blocking collectives, shards(): lax.all_to_all(repeat(tokens, members), ALL, 0, 0, axis_index_groups=far)  29.4 us
    all_to_all x1, blocking collectives, shards(): lax.all_to_all(total.astype(bf16).reshape(members, own, width), ALL, 0, 0...  21.1 us
    all_to_all x1, blocking collectives, shards(): lax.all_to_all(repeat(mine, 4), ALL, 0, 0, axis_index_groups=near)  16.5 us
    all_to_all x1, blocking collectives, shards(): lax.all_to_all(outs.reshape(4, quarter, width), ALL, 0, 0, axis_index_gro...  16.4 us
    ppermute x2, waiting for transfers between devices, swap_chips(): return lax.ppermute(x, 'depth', pairs)  15.4 us
    ppermute x2, starting transfers between devices, swap_chips(): return lax.ppermute(x, 'depth', pairs)  5.12 us
    ppermute x2, starting transfers between devices, swap_cores(): lax.ppermute(x, 'depth', [(d, d ^ 1) for d in range(lax.axis_size('depth'...  3.84 us
    ppermute x2, waiting for transfers between devices, swap_cores(): lax.ppermute(x, 'depth', [(d, d ^ 1) for d in range(lax.axis_size('depth'...  2.36 us
  transfers between devices with their start and end apart: 4, of which 4 were waited for; matrix products, arithmetic and copies ran while one was open for 1% of the time, Pallas kernels for 0%

profile of v5, /device:TPU:6, one launch (start us, length us, event | category | flops | bytes accessed | tf_op | source)
XLA Modules:
  0.0 116.6 jit_solution(7641911545519342739)
XLA Ops:
  0.0 0.0 copy-start
  0.0 0.9 broadcast_in_dim.6
  0.9 29.4 %all_to_all.20 = bf16[16,8,1536]{2,1,0:T(8,128)(2,1)S(1)} all-to-all(bf16[16,8,1536]{2,1,0:T(8,128)(2,1)S(1)} %broadcast_in_dim.6), channel_id=1, replica_groups={{0,16,32,48,128,144,160,176,432,416,400,384,304,288,272,256},{8,24,40,5..., dimensions={0} | all-to-all | bytes 786432 | tf_op jit(solution)/shard_map/all_to_all | solution.py:61
  30.4 0.0 copy-start.3
  30.4 0.1 broadcast_in_dim.8
  30.5 16.5 %all_to_all.21 = bf16[4,128,1536]{2,1,0:T(8,128)(2,1)S(1)} all-to-all(bf16[4,128,1536]{2,1,0:T(8,128)(2,1)S(1)} %broadcast_in_dim.8), channel_id=1, replica_groups={{16,72,8,80},{32,88,24,96},{48,104,40,112},{0,120,56,64},{144,200,136,2..., dimensions={0} | all-to-all | bytes 3145728 | tf_op jit(solution)/shard_map/all_to_all | solution.py:62
  47.0 0.0 copy-done.3
  47.0 0.8 fusion.4
  47.8 1.9 %collective-permute-start = (f32[4,64,768]{2,1,0:T(8,128)S(1)}, f32[4,64,768]{2,1,0:T(8,128)S(1)}, u32[]{:S(2)}, u32[]{:S(2)}) collective-permute-start(f32[4,64,768]{2,1,0:T(8,128)S(1)} %fusion.4), channel_id=1, source_target_pairs={{0,1},{1,0},{2,3},{3,2},{4,5},{5,4},{6,7},{7,6},{8,9},{9,8},{10,11... | collective-permute-start | bytes 2359304 | tf_op jit(solution)/shard_map/ppermute | solution.py:33
  49.7 0.8 fusion.6
  50.5 0.0 copy-start.2
  50.5 1.5 %collective-permute-done = f32[4,64,768]{2,1,0:T(8,128)S(1)} collective-permute-done((f32[4,64,768]{2,1,0:T(8,128)S(1)}, f32[4,64,768]{2,1,0:T(8,128)S(1)}, u32[]{:S(2)}, u32[]{:S(2)}) %collective-permute-start) | collective-permute-done | bytes 786464 | tf_op jit(solution)/shard_map/ppermute | solution.py:33
  52.0 0.1 fusion.20
  52.1 2.7 %collective-permute-start.1 = (bf16[4,64,768]{2,1,0:T(8,128)(2,1)S(1)}, bf16[4,64,768]{2,1,0:T(8,128)(2,1)S(1)}, u32[]{:S(2)}, u32[]{:S(2)}) collective-permute-start(bf16[4,64,768]{2,1,0:T(8,128)(2,1)S(1)} %get-tuple-element.9), channel_id=1, source_target_pairs={{0,2},{1,7},{2,0},{3,5},{4,6},{5,3},{6,4},{7,1},{8,10},{9,15},{10,... | collective-permute-start | bytes 1179656 | tf_op jit(solution)/shard_map/ppermute | solution.py:43
  54.8 6.9 %collective-permute-done.1 = bf16[4,64,768]{2,1,0:T(8,128)(2,1)S(1)} collective-permute-done((bf16[4,64,768]{2,1,0:T(8,128)(2,1)S(1)}, bf16[4,64,768]{2,1,0:T(8,128)(2,1)S(1)}, u32[]{:S(2)}, u32[]{:S(2)}) %collective-permute-start.1) | collective-permute-done | bytes 393248 | tf_op jit(solution)/shard_map/ppermute | solution.py:43
  61.8 0.1 fusion.18
  61.8 2.4 %collective-permute-start.2 = (bf16[4,64,768]{2,1,0:T(8,128)(2,1)S(1)}, bf16[4,64,768]{2,1,0:T(8,128)(2,1)S(1)}, u32[]{:S(2)}, u32[]{:S(2)}) collective-permute-start(bf16[4,64,768]{2,1,0:T(8,128)(2,1)S(1)} %fusion.18), channel_id=1, source_target_pairs={{0,6},{1,3},{2,4},{3,1},{4,2},{5,7},{6,0},{7,5},{8,14},{9,11},{10,... | collective-permute-start | bytes 1179656 | tf_op jit(solution)/shard_map/ppermute | solution.py:43
  64.2 8.5 %collective-permute-done.2 = bf16[4,64,768]{2,1,0:T(8,128)(2,1)S(1)} collective-permute-done((bf16[4,64,768]{2,1,0:T(8,128)(2,1)S(1)}, bf16[4,64,768]{2,1,0:T(8,128)(2,1)S(1)}, u32[]{:S(2)}, u32[]{:S(2)}) %collective-permute-start.2) | collective-permute-done | bytes 393248 | tf_op jit(solution)/shard_map/ppermute | solution.py:43
  72.7 0.0 copy-done.2
  72.7 0.4 fusion.15
  73.1 1.9 %collective-permute-start.3 = (bf16[4,64,768]{2,1,0:T(8,128)(2,1)S(1)}, bf16[4,64,768]{2,1,0:T(8,128)(2,1)S(1)}, u32[]{:S(2)}, u32[]{:S(2)}) collective-permute-start(bf16[4,64,768]{2,1,0:T(8,128)(2,1)S(1)} %fusion.15), channel_id=1, source_target_pairs={{0,1},{1,0},{2,3},{3,2},{4,5},{5,4},{6,7},{7,6},{8,9},{9,8},{10,11... | collective-permute-start | bytes 1179656 | tf_op jit(solution)/shard_map/ppermute | solution.py:33
  75.0 0.0 copy-done
  75.0 0.8 fusion
  75.8 0.9 collective-permute-done.3
  76.7 0.8 fusion.1
  77.5 0.1 pad_maximum_fusion
  77.7 0.1 copy.8
  77.8 16.4 %all_to_all.22 = bf16[4,128,1536]{2,1,0:T(8,128)(2,1)S(1)} all-to-all(bf16[4,128,1536]{2,1,0:T(8,128)(2,1)S(1)} %bitcast.31), channel_id=1, replica_groups={{16,72,8,80},{32,88,24,96},{48,104,40,112},{0,120,56,64},{144,200,136,2..., dimensions={0} | all-to-all | bytes 3145728 | tf_op jit(solution)/shard_map/all_to_all | solution.py:76
  94.2 0.4 convert_element_type.44
  94.6 0.0 copy-start.1
  94.6 0.2 fusion.19
  94.8 21.1 %all_to_all.23 = bf16[16,8,1536]{2,1,0:T(8,128)(2,1)S(1)} all-to-all(bf16[16,8,1536]{2,1,0:T(8,128)(2,1)S(1)} %fusion.19), channel_id=1, replica_groups={{0,16,32,48,128,144,160,176,432,416,400,384,304,288,272,256},{8,24,40,5..., dimensions={0} | all-to-all | bytes 786432 | tf_op jit(solution)/shard_map/all_to_all | solution.py:77
  115.9 0.1 convert_reduce_fusion
  116.0 0.0 copy-done.1
  116.0 0.6 add_convert_fusion
Async XLA Ops:
  0.0 75.0 %copy-start = (bf16[768,1536]{1,0:T(8,128)(2,1)S(1)}, bf16[768,1536]{1,0:T(8,128)(2,1)}, u32[]{:S(2)}) copy-start(bf16[768,1536]{1,0:T(8,128)(2,1)} %param.8) | copy-start | bytes 7077892
  30.4 16.7 %copy-start.3 = (bf16[1536,768]{1,0:T(8,128)(2,1)S(1)}, bf16[1536,768]{1,0:T(8,128)(2,1)}, u32[]{:S(2)}) copy-start(bf16[1536,768]{1,0:T(8,128)(2,1)} %param.6) | copy-start | bytes 7077892
  47.8 4.2 %collective-permute-start = (f32[4,64,768]{2,1,0:T(8,128)S(1)}, f32[4,64,768]{2,1,0:T(8,128)S(1)}, u32[]{:S(2)}, u32[]{:S(2)}) collective-permute-start(f32[4,64,768]{2,1,0:T(8,128)S(1)} %fusion.4), channel_id=1, source_target_pairs={{0,1},{1,0},{2,3},{3,2},{4,5},{5,4},{6,7},{7,6},{8,9},{9,8},{10,11... | collective-permute-start | bytes 2359304 | tf_op jit(solution)/shard_map/ppermute | solution.py:33
  50.5 22.2 %copy-start.2 = (f32[768]{0:T(1024)S(1)}, f32[768]{0:T(1024)}, u32[]{:S(2)}) copy-start(f32[768]{0:T(1024)} %param.7) | copy-start | bytes 9220
  52.1 9.7 %collective-permute-start.1 = (bf16[4,64,768]{2,1,0:T(8,128)(2,1)S(1)}, bf16[4,64,768]{2,1,0:T(8,128)(2,1)S(1)}, u32[]{:S(2)}, u32[]{:S(2)}) collective-permute-start(bf16[4,64,768]{2,1,0:T(8,128)(2,1)S(1)} %get-tuple-element.9), channel_id=1, source_target_pairs={{0,2},{1,7},{2,0},{3,5},{4,6},{5,3},{6,4},{7,1},{8,10},{9,15},{10,... | collective-permute-start | bytes 1179656 | tf_op jit(solution)/shard_map/ppermute | solution.py:43
  61.8 10.9 %collective-permute-start.2 = (bf16[4,64,768]{2,1,0:T(8,128)(2,1)S(1)}, bf16[4,64,768]{2,1,0:T(8,128)(2,1)S(1)}, u32[]{:S(2)}, u32[]{:S(2)}) collective-permute-start(bf16[4,64,768]{2,1,0:T(8,128)(2,1)S(1)} %fusion.18), channel_id=1, source_target_pairs={{0,6},{1,3},{2,4},{3,1},{4,2},{5,7},{6,0},{7,5},{8,14},{9,11},{10,... | collective-permute-start | bytes 1179656 | tf_op jit(solution)/shard_map/ppermute | solution.py:43
  73.1 3.6 %collective-permute-start.3 = (bf16[4,64,768]{2,1,0:T(8,128)(2,1)S(1)}, bf16[4,64,768]{2,1,0:T(8,128)(2,1)S(1)}, u32[]{:S(2)}, u32[]{:S(2)}) collective-permute-start(bf16[4,64,768]{2,1,0:T(8,128)(2,1)S(1)} %fusion.15), channel_id=1, source_target_pairs={{0,1},{1,0},{2,3},{3,2},{4,5},{5,4},{6,7},{7,6},{8,9},{9,8},{10,11... | collective-permute-start | bytes 1179656 | tf_op jit(solution)/shard_map/ppermute | solution.py:33
  94.6 21.4 %copy-start.1 = (f32[1536]{0:T(1024)S(1)}, f32[1536]{0:T(1024)}, u32[]{:S(2)}) copy-start(f32[1536]{0:T(1024)} %param.9) | copy-start | bytes 18436
